TPU v7x, 32 devices: a whole 2x2x4 slice. The times are simulated.
32 devices in a mesh: dp: 2 (over x), seq: 16 (over z, y, core).
Axes of the slice: x: 2, y: 2, z: 4, core: 2. Of those that a mesh axis runs over, the one named last changes fastest.
Arguments:
- inputs: float32 [2, 2048, 2048], P('dp', 'seq'), may hold values from -6 to 6
- cotangent: float32 [2, 2048, 2048], P('dp', 'seq'), may hold values from -6 to 6
- block_mix: float32 [128, 128], replicated, may hold values from -0.5 to 0.5
- twist_hi: float32 [2, 2, 2048], replicated, may hold values from -3 to 3
- twist_lo: float32 [2, 2, 2048], replicated, may hold values from -3 to 3
- gain: float32 [2048], replicated, may hold values from 0.5 to 1.5
- gate_up: float32 [128, 2, 16, 256], P('seq'), may hold values from -0.5 to 0.5
- down: float32 [256, 16, 128], P('seq'), may hold values from -0.375 to 0.375
Outputs:
- grad_inputs: float32 [2, 2048, 2048], P('dp', 'seq')
- grad_gate_up: float32 [128, 2, 16, 256], P('seq')
- grad_down: float32 [256, 16, 128], P('seq')
- grad_block_mix: float32 [128, 128], replicated
- grad_twist_hi: float32 [2, 2, 2048], replicated
- grad_twist_lo: float32 [2, 2, 2048], replicated
- grad_gain: float32 [2048], replicated
All inputs are finite; a program needn't handle non-finite values.
Results may differ from a plain program's by a relative error of at most 0.00022.
Values sent between devices are 32-bit elements; how exact they have to be, the bound alone decides.
A program may use at most 64 MiB of HBM per device.

v0:
```python
import math

import jax
import jax.numpy as jnp
from jax import lax
from jax.sharding import PartitionSpec as P

NB = 16
BLK = 128
DB = 128


HIGH = lax.Precision.HIGHEST
EPS = 1e-05


def from_partner(block, axis, distance):
    count = lax.axis_size(axis)
    route = []
    for low in range(count):
        high = low | 1 << distance
        if high != low and high < count:
            route += [(low, high), (high, low)]
    return lax.ppermute(block, axis, route)


def side_of(bit):
    return lax.axis_index("seq") // (1 << bit) % 2


def forward_section(field, coeff, bit):
    partner = from_partner(field, "seq", bit)
    own = coeff[side_of(bit)]
    return (own[0] * field + own[1] * partner, partner)


def backward_section(grad, field, partner, coeff, bit):
    side = side_of(bit)
    own = coeff[side]
    sent = from_partner(own[1] * grad, "seq", bit)
    back = own[0] * grad + sent
    term = jnp.stack([jnp.sum(grad * field, axis=0), jnp.sum(grad * partner, axis=0)])
    pick = (jnp.arange(2) == side).astype(jnp.float32)
    return (back, pick[:, None, None] * term[None])


def per_device(inputs, cotangent, block_mix, twist_hi, twist_lo, gain, gate_up, down):
    seq_in = inputs[0]
    tokens, width = seq_in.shape
    count = lax.axis_size("seq")
    top_bit = count.bit_length() - 2
    nblocks = tokens // BLK
    xb = seq_in.reshape(nblocks, BLK, width)
    mixed = jnp.einsum("ij,kjd->kid", block_mix, xb, precision=HIGH).reshape(tokens, width)
    first, mixed_peer = forward_section(mixed, twist_hi, top_bit)
    second, first_peer = forward_section(first, twist_lo, 0)
    resid = seq_in + second
    scale = lax.rsqrt(jnp.mean(resid * resid, axis=-1, keepdims=True) + EPS)
    unit = resid * scale
    normed = (unit * gain).reshape(tokens, NB, DB)
    full_gu, full_down = (
        lax.all_gather(gate_up, "seq", axis=0, tiled=True),
        lax.all_gather(down, "seq", axis=0, tiled=True),
    )
    gate_val = jnp.einsum("tnd,dnf->tnf", normed, full_gu[:, 0], precision=HIGH)
    up_val = jnp.einsum("tnd,dnf->tnf", normed, full_gu[:, 1], precision=HIGH)
    sig = jax.nn.sigmoid(gate_val)
    act = gate_val * sig
    hidden = act * up_val
    grad_out = cotangent[0]
    grad_blocks = grad_out.reshape(tokens, NB, DB)
    grad_hidden = jnp.einsum("tnd,fnd->tnf", grad_blocks, full_down, precision=HIGH)
    grad_gate = grad_hidden * up_val * sig * (1.0 + gate_val * (1.0 - sig))
    grad_up = grad_hidden * act
    grad_normed = jnp.einsum("tnf,dnf->tnd", grad_gate, full_gu[:, 0], precision=HIGH)
    grad_normed = grad_normed + jnp.einsum("tnf,dnf->tnd", grad_up, full_gu[:, 1], precision=HIGH)
    grad_normed = grad_normed.reshape(tokens, width)
    cols = normed
    whole_gu = jnp.stack(
        [
            jnp.einsum("tnd,tnf->dnf", cols, grad_gate, precision=HIGH),
            jnp.einsum("tnd,tnf->dnf", cols, grad_up, precision=HIGH),
        ],
        axis=1,
    )
    cols = hidden
    whole_down = jnp.einsum("tnf,tnd->fnd", cols, grad_blocks, precision=HIGH)
    whole_gu, whole_down = lax.psum((whole_gu, whole_down), "dp")
    part_gu, part_down = (
        lax.psum_scatter(whole_gu, "seq", scatter_dimension=0, tiled=True),
        lax.psum_scatter(whole_down, "seq", scatter_dimension=0, tiled=True),
    )
    grad_gain_local = jnp.sum(grad_normed * unit, axis=0)
    weighted = grad_normed * gain
    inner = jnp.mean(weighted * resid, axis=-1, keepdims=True)
    grad_resid = grad_out + scale * weighted - resid * scale * scale * scale * inner
    grad_first, term_lo = backward_section(grad_resid, first, first_peer, twist_lo, 0)
    grad_mixed, term_hi = backward_section(grad_first, mixed, mixed_peer, twist_hi, top_bit)
    grad_mb = grad_mixed.reshape(nblocks, BLK, width)
    term_block = jnp.einsum("kid,kjd->ij", grad_mb, xb, precision=HIGH)
    grad_seq = jnp.einsum("ij,kid->kjd", block_mix, grad_mb, precision=HIGH).reshape(tokens, width)
    grad_seq = grad_seq + grad_resid
    sum_block, sum_hi, sum_lo, sum_gain = lax.psum(
        (term_block, term_hi, term_lo, grad_gain_local), ("dp", "seq")
    )
    factor = 1.0 / math.sqrt(lax.axis_size("dp") * count * tokens)
    return (
        grad_seq[None],
        part_gu * factor,
        part_down * factor,
        sum_block * factor,
        sum_hi * factor,
        sum_lo * factor,
        sum_gain * factor,
    )


def solution(mesh):
    return jax.shard_map(
        per_device,
        mesh=mesh,
        in_specs=(
            P("dp", "seq", None),
            P("dp", "seq", None),
            P(),
            P(),
            P(),
            P(),
            P("seq", None, None, None),
            P("seq", None, None),
        ),
        out_specs=(
            P("dp", "seq", None),
            P("seq", None, None, None),
            P("seq", None, None),
            P(),
            P(),
            P(),
            P(),
        ),
        check_vma=False,
    )
```

profile of v0, /device:TPU:0, one launch (start us, length us, event | category | flops | bytes accessed | tf_op | source)
XLA Modules:
  0.0 599.4 jit_solution(11755261424137522082)
XLA Ops:
  7.2 1.6 copy.34
  8.9 1.8 copy.36
  10.8 3.0 convolution_bitcast_fusion.1
  13.9 4.1 collective-permute-start
  18.0 57.8 %collective-permute-done = f32[128,2048]{0,1:T(8,128)S(1)} collective-permute-done((f32[128,2048]{0,1:T(8,128)S(1)}, f32[128,2048]{0,1:T(8,128)S(1)}, u32[]{:S(2)}, u32[]{:S(2)}) %collective-permute-start) | collective-permute-done | bytes 1048608 | tf_op jit(solution)/shard_map/ppermute | solution.py:24
  75.8 1.0 copy-done.7
  76.8 1.9 multiply_add_fusion.2
  78.8 1.3 copy.33
  80.1 2.7 copy.32
  83.0 1.3 copy-done.10
  84.3 1.9 multiply_reduce_fusion.5
  86.3 0.3 multiply_multiply_fusion
  86.7 5.2 fusion.21
  91.8 42.3 %all-gather.5.cloned.1.call-done = f32[128,2,16,256]{3,0,2,1:T(8,128)} async-done(((f32[8,2,16,256]{3,0,2,1:T(8,128)}), f32[128,2,16,256]{3,0,2,1:T(8,128)}) %all-gather.5.cloned.1.call-update) | async-done | bytes 4194320 | tf_op jit(solution)/shard_map/all_gather | solution.py:62
  134.1 5.5 fusion.12
  139.6 3.7 fusion.10
  143.3 3.3 fusion.9
  146.6 3.3 fusion.14
  150.0 1.3 fusion.18
  151.5 2.2 multiply_reduce_fusion.1
  153.7 0.3 broadcast_multiply_fusion
  154.0 0.3 collective-permute-start.2
  154.4 0.7 broadcast_multiply_fusion.5
  155.1 1.7 collective-permute-done.2
  156.8 0.9 multiply_reduce_fusion.3
  157.7 0.7 broadcast_multiply_fusion.8
  158.5 6.4 %fusion.13 = f32[256,16,128]{2,0,1:T(8,128)} fusion(f32[16,128,256]{1,2,0:T(8,128)} %copy-done.18, f32[128,16,128]{2,1,0:T(8,128)} %bitcast.136, f32[16,128,256]{1,2,0:T(8,128)} %copy-done.16), kind=kOutput, calls=%fused_computation.24 | convolution fusion | flops 807927808 | bytes 7340032 | tf_op jit(solution)/shard_map/tnf,tnd->fnd/dot_general | solution.py:87
  165.0 4.6 convolution_bitcast_fusion.2
  169.6 2.6 convolution_bitcast_fusion.3
  172.2 2.5 pad_maximum_fusion
  174.7 5.5 copy.45
  180.3 1.3 broadcast_multiply_fusion.1
  181.6 1.5 collective-permute-start.3
  183.1 110.5 %all-reduce.8.cloned.1.call-done = (f32[2,2,2048]{2,1,0:T(2,128)}, f32[2,2,2048]{2,1,0:T(2,128)}, f32[2048]{0:T(1024)}) async-done(((f32[2,2,2048]{2,1,0:T(2,128)}, f32[2,2,2048]{2,1,0:T(2,128)}, f32[2048]{0:T(1024)}), (f32[2,2,2048]{2,1,0:T(2,128)}, f32[2,2,2048]{2,1,0:T(2,128)}, f32[2048]{0:T(1024)})) %all-reduce.8.cloned.1.call-update) | async-done | bytes 73744 | tf_op jit(solution)/shard_map/psum | solution.py:103
  293.6 1.4 broadcast_multiply_fusion.6
  295.0 1.4 broadcast_multiply_fusion.7
  296.4 4.0 fusion.15
  300.5 0.6 broadcast_multiply_fusion.9
  301.1 60.5 %reduce-scatter.5.cloned.1.call-done = f32[16,16,128]{2,0,1:T(8,128)} async-done(((f32[256,16,128]{2,0,1:T(8,128)}), f32[16,16,128]{2,0,1:T(8,128)}) %reduce-scatter.5.cloned.1.call-update) | async-done | bytes 131088 | tf_op jit(solution)/shard_map/reduce_scatter | solution.py:91
  361.6 76.0 %reduce-scatter.3.cloned.1.call-done = f32[8,2,16,256]{3,2,1,0:T(8,128)} async-done(((f32[128,2,16,256]{3,2,1,0:T(8,128)}), f32[8,2,16,256]{3,2,1,0:T(8,128)}) %reduce-scatter.3.cloned.1.call-update) | async-done | bytes 262160 | tf_op jit(solution)/shard_map/reduce_scatter | solution.py:90
  437.6 2.2 fusion.1
  439.9 1.3 copy.47
  441.2 119.0 %all-reduce.6.cloned.1.call-done = f32[128,128]{1,0:T(8,128)} async-done(((f32[128,128]{1,0:T(8,128)}), f32[128,128]{1,0:T(8,128)}) %all-reduce.6.cloned.1.call-update) | async-done | bytes 65552 | tf_op jit(solution)/shard_map/psum | solution.py:103
  560.2 1.5 broadcast_multiply_fusion.4
  561.6 27.7 %all-reduce.10.cloned.1.call-done = (f32[8,2,16,256]{3,2,1,0:T(8,128)}, f32[16,16,128]{2,0,1:T(8,128)}) async-done(((f32[8,2,16,256]{3,2,1,0:T(8,128)}, f32[16,16,128]{2,0,1:T(8,128)}), (f32[8,2,16,256]{3,2,1,0:T(8,128)}, f32[16,16,128]{2,0,1:T(8,128)})) %all-reduce.10.cloned.1.call-update) | async-done | bytes 393232 | tf_op jit(solution)/shard_map/psum | solution.py:88
  589.3 1.7 broadcast_multiply_fusion.2
  591.0 0.9 broadcast_multiply_fusion.3
  591.9 0.7 copy.48
  (72 shorter events, 1.1 us)
Async XLA Ops:
  7.2 3.6 copy-start
  7.2 10.8 %copy-start.23 = (f32[2,2,2048]{2,1,0:T(2,128)S(1)}, f32[2,2,2048]{2,1,0:T(2,128)}, u32[]{:S(2)}) copy-start(f32[2,2,2048]{2,1,0:T(2,128)} %param.11) | copy-start | bytes 98308
  7.2 10.8 %copy-start.22 = (f32[2,2,2048]{2,1,0:T(2,128)S(1)}, f32[2,2,2048]{2,1,0:T(2,128)}, u32[]{:S(2)}) copy-start(f32[2,2,2048]{2,1,0:T(2,128)} %param.12) | copy-start | bytes 98308
  7.2 79.4 %all-gather.3.cloned.1.call-start = ((), (), s32[]{:S(2)}) async-start(), calls=%async_computation.2 | async-start | bytes 2228224 | tf_op jit(solution)/shard_map/all_gather | solution.py:63
  8.9 125.2 %all-gather.5.cloned.1.call-start = ((), (), s32[]{:S(2)}) async-start(), calls=%async_computation.3 | async-start | bytes 4456448 | tf_op jit(solution)/shard_map/all_gather | solution.py:62
  10.8 282.8 %all-reduce.8.cloned.1.call-start = ((), (), s32[]{:S(2)}) async-start(), calls=%async_computation.7 | async-start | bytes 147456 | tf_op jit(solution)/shard_map/psum | solution.py:103
  13.9 66.3 %copy-start.1 = (f32[128,2048]{0,1:T(8,128)}, f32[128,2048]{0,1:T(8,128)S(1)}, u32[]{:S(2)}) copy-start(f32[128,2048]{0,1:T(8,128)S(1)} %convolution_bitcast_fusion.1) | copy-start | bytes 3145732
  13.9 64.9 %copy-start.3 = (f32[1,128,2048]{2,1,0:T(8,128)S(1)}, f32[1,128,2048]{2,1,0:T(8,128)}, u32[]{:S(2)}) copy-start(f32[1,128,2048]{2,1,0:T(8,128)} %param.8) | copy-start | bytes 3145732
  13.9 61.9 %collective-permute-start = (f32[128,2048]{0,1:T(8,128)S(1)}, f32[128,2048]{0,1:T(8,128)S(1)}, u32[]{:S(2)}, u32[]{:S(2)}) collective-permute-start(f32[128,2048]{0,1:T(8,128)S(1)} %convolution_bitcast_fusion.1), channel_id=1, source_target_pairs={{0,8},{8,0},{1,9},{9,1},{2,10},{10,2},{3,11},{11,3},{4,12},{12,4},... | collective-permute-start | bytes 3145736 | tf_op jit(solution)/shard_map/ppermute | solution.py:24
  75.8 1.0 copy-start.7
  78.7 4.3 copy-start.5
  78.7 4.3 collective-permute-start.1
  80.1 2.7 copy-start.12
  82.8 1.5 copy-start.10
  83.0 3.6 copy-start.9
  84.3 2.0 copy-start.20
  134.1 5.5 copy-start.11
  139.6 7.0 %copy-start.16 = (f32[16,128,256]{1,2,0:T(8,128)}, f32[16,128,256]{1,2,0:T(8,128)S(1)}, u32[]{:S(2)}) copy-start(f32[16,128,256]{1,2,0:T(8,128)S(1)} %fusion.12) | copy-start | bytes 6291460
  139.6 3.7 copy-start.14
  143.3 3.3 copy-start.18
  150.0 1.3 copy-start.6
  150.0 1.5 copy-start.13
  153.7 3.1 copy-start.2
  153.7 3.1 copy-start.8
  154.0 2.7 collective-permute-start.2
  158.5 203.1 %reduce-scatter.5.cloned.1.call-start = ((), (), s32[]{:S(2)}) async-start(), calls=%async_computation.6 | async-start | bytes 2228224 | tf_op jit(solution)/shard_map/reduce_scatter | solution.py:91
  164.9 272.7 %reduce-scatter.3.cloned.1.call-start = ((), (), s32[]{:S(2)}) async-start(), calls=%async_computation.5 | async-start | bytes 4456448 | tf_op jit(solution)/shard_map/reduce_scatter | solution.py:90
  165.0 4.6 copy-start.15
  165.0 4.6 copy-start.17
  165.0 4.6 copy-start.19
  180.2 116.2 %copy-start.4 = (f32[1,128,2048]{2,1,0:T(8,128)S(1)}, f32[1,128,2048]{2,1,0:T(8,128)}, u32[]{:S(2)}) copy-start(f32[1,128,2048]{2,1,0:T(8,128)} %param.8) | copy-start | bytes 3145732
  180.2 380.0 %all-reduce.6.cloned.1.call-start = ((), (), s32[]{:S(2)}) async-start(), calls=%async_computation.4 | async-start | bytes 131072 | tf_op jit(solution)/shard_map/psum | solution.py:103
  181.6 114.8 %collective-permute-start.3 = (f32[128,2048]{0,1:T(8,128)}, f32[128,2048]{0,1:T(8,128)}, u32[]{:S(2)}, u32[]{:S(2)}) collective-permute-start(f32[128,2048]{0,1:T(8,128)} %broadcast_multiply_fusion.1), channel_id=1, source_target_pairs={{0,8},{8,0},{1,9},{9,1},{2,10},{10,2},{3,11},{11,3},{4,12},{12,4},... | collective-permute-start | bytes 3145736 | tf_op jit(solution)/shard_map/ppermute | solution.py:24
  293.6 6.9 %copy-start.21 = (f32[2048]{0:T(1024)S(1)}, f32[2048]{0:T(1024)}, u32[]{:S(2)}) copy-start(f32[2048]{0:T(1024)} %get-tuple-element.29) | copy-start | bytes 24580
  300.4 288.9 %all-reduce.10.cloned.1.call-start = ((), (), s32[]{:S(2)}) async-start(), calls=%async_computation.8 | async-start | bytes 786432 | tf_op jit(solution)/shard_map/psum | solution.py:88
Sparse Core Ops, SparseCore 0:
  10.8 67.4 all-gather.2
  81.0 53.0 all-gather.4
  158.6 134.9 all-reduce.7
  297.2 64.3 reduce-scatter.4
  365.8 71.7 reduce-scatter.2
  443.6 116.5 all-reduce.5
  562.6 26.7 all-reduce.9
where the time goes:
time: 600 us; the launch traced here: 599 us
  waiting for transfers between devices  496 us (83%)
  matrix products  43.8 us (7%)
  other arithmetic  21.6 us (4%)
  local copies, waits for them, and re-layouts  17.7 us (3%)
  between operations  14.5 us (2%)
  starting transfers between devices  6.27 us (1%)
    psum x2, waiting for transfers between devices, per_device(): lax.psum((term_block, term_hi, term_lo, grad_gain_local), ('dp', 'seq'))  230 us
    reduce_scatter x1, waiting for transfers between devices, per_device(): lax.psum_scatter(whole_gu, 'seq', scatter_dimension=0, tiled=True)  76 us
    reduce_scatter x1, waiting for transfers between devices, per_device(): lax.psum_scatter(whole_down, 'seq', scatter_dimension=0, tiled=True)  60.5 us
    ppermute x4, waiting for transfers between devices, from_partner(): return lax.ppermute(block, axis, route)  59.5 us
    all_gather x1, waiting for transfers between devices, per_device(): lax.all_gather(gate_up, 'seq', axis=0, tiled=True)  42.3 us
    psum x1, waiting for transfers between devices, per_device(): whole_gu, whole_down = lax.psum((whole_gu, whole_down), 'dp')  27.7 us
    unnamed x55, local copies, waits for them, and re-layouts  12.2 us
  transfers between devices with their start and end apart: 11, of which 8 were waited for; matrix products, arithmetic and copies ran while one was open for 9% of the time, Pallas kernels for 0%

commit v1 on v0

v1 whole, which is shorter than its diff:
```python
import functools
import math

import jax
import jax.numpy as jnp
from jax import lax
from jax.experimental import pallas as pl
from jax.experimental.pallas import tpu as pltpu
from jax.sharding import PartitionSpec as P

NB = 16
BLK = 128
DB = 128
FB = 256
EPS = 1e-05
SMALL = 16
F32 = jnp.float32
BF16 = jnp.bfloat16
NN = (((1,), (0,)), ((), ()))
NT = (((1,), (1,)), ((), ()))
TN = (((0,), (0,)), ((), ()))
ORDER = (8, 4, 9, 12, 1, 13, 10, 5, 14, 2, 11, 6, 15, 3, 7)


def xor(a, b, bits):
    total = a + b
    for bit in range(bits):
        total = total - 2 * (1 << bit) * ((a // (1 << bit)) % 2) * ((b // (1 << bit)) % 2)
    return total


def split(value):
    high = value.astype(BF16)
    return high, (value - high.astype(F32)).astype(BF16)


def dot(a, b, dims):
    return lax.dot_general(a, b, dims, preferred_element_type=F32)


def left(value, axis):
    high, low = split(value)
    return jnp.concatenate([high, low, high], axis=axis)


def right(value, axis):
    high, low = split(value)
    return jnp.concatenate([high, high, low], axis=axis)


def row_sums(value):
    high, low = split(value)
    ones = jnp.ones((8, 2 * value.shape[1]), BF16)
    return dot(ones, jnp.concatenate([high, low], axis=1), NT)[0:1]


def as_columns(row):
    return jnp.broadcast_to(row, (DB, row.shape[1])).T


def arrived(ref, sem):
    pltpu.make_async_copy(ref, ref, sem).wait()


def kernel(
    dps, count, factor,
    x_hbm, g_hbm, gu_hbm, dn_hbm, bm_ref, th_ref, tl_ref, gain_ref,
    out_x, out_gu, out_dn, out_small,
    xb, gb, mixed, first, resid, scb, wsc, gseq,
    gu_in, dn_in, gu_f32, dn_f32, gu_k, gu_n, dn_n,
    gu_rep, dn_rep, gu_out, dn_out, sm_rep, sm_tot, bm_in, pack,
    ss_buf, in_buf, rows_ref,
    x_s, x_r, g_s, g_r, gu_s, gu_r, dn_s, dn_r, ss_s, ss_r, in_s, in_r,
    o_s, o_r, gr_s, gr_r, dr_s, dr_r, go_s, go_r, do_s, do_r, sr_s, sr_r,
    bm_s, bm_r, pk_s, pk_r,
):
    groups = count // NB
    bits = count.bit_length() - 1
    reps = dps * groups
    rows, drows = DB // count, FB // count
    me = lax.axis_index("seq")
    dp = lax.axis_index("dp")
    rank = me % 2 + me // (2 * groups) * 2
    group = me // 2 % groups
    rep = dp * groups + group

    def seq_of(rk, grp):
        return rk % 2 + grp * 2 + rk // 2 * 2 * groups

    def peer(k):
        return seq_of(xor(rank, k, 4), group)

    def send(src, dst, ssem, rsem, to_dp, to_seq):
        copy = pltpu.make_async_remote_copy(
            src_ref=src, dst_ref=dst, send_sem=ssem, recv_sem=rsem,
            device_id=(to_dp, to_seq), device_id_type=pl.DeviceIdType.MESH,
        )
        copy.start()
        return copy

    def cols(ref, rk):
        return ref.at[:, pl.ds(pl.multiple_of(rk * DB, DB), DB)]

    replicas = []
    for step in range(1, reps):
        other = (rep + step) % reps
        replicas.append((step, other, other // groups, seq_of(rank, other % groups)))

    barrier = pltpu.get_barrier_semaphore()
    met = 0
    for k in range(1, count):
        pl.semaphore_signal(
            barrier, inc=1, device_id=(dp, xor(me, k, bits)), device_id_type=pl.DeviceIdType.MESH
        )
        met += 1
    for step in range(1, dps):
        for grp in range(groups):
            pl.semaphore_signal(
                barrier, inc=1, device_id=((dp + step) % dps, seq_of(rank, grp)),
                device_id_type=pl.DeviceIdType.MESH,
            )
            met += 1
    pl.semaphore_wait(barrier, met)

    sent = []
    local = [
        pltpu.make_async_copy(cols(x_hbm, rank), xb.at[0], x_r.at[0]),
        pltpu.make_async_copy(cols(g_hbm, rank), gb.at[0], g_r.at[0]),
        pltpu.make_async_copy(gu_hbm.at[rank], gu_in.at[me], gu_r.at[0]),
        pltpu.make_async_copy(dn_hbm.at[rank], dn_in.at[me], dn_r.at[0]),
    ]
    for copy in local:
        copy.start()
    for k in ORDER:
        sent.append(send(cols(x_hbm, xor(rank, k, 4)), xb.at[k], x_s.at[k], x_r.at[k], dp, peer(k)))
    for j in range(1, count):
        k = ORDER[j - 1] if count == NB else j
        to = xor(me, k, bits)
        block = to % 2 + to // (2 * groups) * 2
        sent.append(send(gu_hbm.at[block], gu_in.at[me], gu_s.at[k], gu_r.at[k], dp, to))
        sent.append(send(dn_hbm.at[block], dn_in.at[me], dn_s.at[k], dn_r.at[k], dp, to))

    mix_left = left(bm_ref[...], 1)
    back_left = left(bm_ref[...].T, 1)

    def mix(k, _):
        arrived(xb.at[k], x_r.at[k])
        mixed[k] = dot(mix_left, right(xb[k], 0), NN)
        return 0

    lax.fori_loop(0, NB // 2, mix, 0)
    for k in ORDER:
        sent.append(send(cols(g_hbm, xor(rank, k, 4)), gb.at[k], g_s.at[k], g_r.at[k], dp, peer(k)))
    lax.fori_loop(NB // 2, NB, mix, 0)

    lanes = pl.ds(pl.multiple_of(rank * DB, DB), DB)
    side_hi, side_lo = rank // 8, rank % 2

    def coefficients(ref, side):
        out = []
        for j in range(2):
            pair = ref[side + j - 2 * side * j, :, lanes]
            out.append((pair[0:1], pair[1:2]))
        return out

    hi = coefficients(th_ref, side_hi)
    lo = coefficients(tl_ref, side_lo)
    gain = gain_ref[:, lanes]

    def forward(i, _):
        ks = [2 * i, 2 * i + 1, 2 * i + 8, 2 * i + 9]
        mx = [mixed[k] for k in ks]
        fs = []
        for n in range(4):
            c = hi[n // 2]
            fs.append(c[0] * mx[n] + c[1] * mx[(n + 2) % 4])
            first[ks[n]] = fs[n]
        for n in range(4):
            c = lo[n % 2]
            r = xb[ks[n]] + (c[0] * fs[n] + c[1] * fs[n + 1 - 2 * (n % 2)])
            resid[ks[n]] = r
            ss_buf[0, pl.ds(xor(rank, ks[n], 4), 1), :] = row_sums(r * r)
        return 0

    lax.fori_loop(0, 4, forward, 0)
    for k in ORDER:
        sent.append(send(ss_buf.at[0], ss_buf.at[k], ss_s.at[k], ss_r.at[k], dp, peer(k)))

    for k in range(count):
        owner = xor(me, k, bits)
        arrived(gu_in.at[owner], gu_r.at[k])
        arrived(dn_in.at[owner], dn_r.at[k])
    for s in range(count):
        gu_f32[s * rows : (s + 1) * rows, :] = gu_in[s]
        dn_f32[s * drows : (s + 1) * drows, :] = dn_in[s]
    gu_k[...] = right(gu_f32[...], 0)
    gu_n[...] = right(gu_f32[...], 1)
    dn_n[...] = right(dn_f32[...], 1)
    gu_rep[rep] = jnp.zeros((DB, 2 * FB), F32)
    dn_rep[rep] = jnp.zeros((DB, FB), F32)

    for k in range(1, NB):
        arrived(ss_buf.at[k], ss_r.at[k])
    total = ss_buf[0]
    for k in range(1, NB):
        total = total + ss_buf[k]
    width = NB * DB
    rows_ref[...] = lax.rsqrt(total * (1.0 / width) + EPS)

    def mlp(i, gain_sum):
        scales, resids, cots = [], [], []
        for j in range(2):
            k = 2 * i + j
            arrived(gb.at[k], g_r.at[k])
            sc = as_columns(rows_ref[pl.ds(xor(rank, k, 4), 1), :])
            scb[k] = sc
            scales.append(sc)
            resids.append(resid[k])
            cots.append(gb[k])
        scale = jnp.concatenate(scales, axis=0)
        res = jnp.concatenate(resids, axis=0)
        cot = jnp.concatenate(cots, axis=0)
        unit = res * scale
        nh, nl = split(unit * gain)
        gh, gl = split(cot)
        gu = dot(jnp.concatenate([nh, nl, nh], axis=1), gu_k[...], NN)
        gate, up = gu[:, :FB], gu[:, FB:]
        sig = 1.0 / (1.0 + jnp.exp(-gate))
        act = gate * sig
        grad_hidden = dot(jnp.concatenate([gh, gl, gh], axis=1), dn_n[...], NT)
        hidden = right(act * up, 0)
        grad_gate = grad_hidden * up * sig * (1.0 + gate * (1.0 - sig))
        both_h, both_l = split(jnp.concatenate([grad_gate, grad_hidden * act], axis=1))
        grad_normed = dot(jnp.concatenate([both_h, both_l, both_h], axis=1), gu_n[...], NT)
        gu_rep[rep] += dot(
            jnp.concatenate([nh, nl, nh], axis=0),
            jnp.concatenate([both_h, both_h, both_l], axis=0), TN,
        )
        dn_rep[rep] += dot(jnp.concatenate([gh, gl, gh], axis=0), hidden, TN)
        weighted = grad_normed * gain
        prod = weighted * res
        ws = weighted * scale
        for j in range(2):
            k = 2 * i + j
            wsc[k] = ws[j * BLK : (j + 1) * BLK]
            in_buf[0, pl.ds(xor(rank, k, 4), 1), :] = row_sums(prod[j * BLK : (j + 1) * BLK])
        return gain_sum + jnp.sum(grad_normed * unit, axis=0, keepdims=True)

    gain_sum = lax.fori_loop(0, NB // 2, mlp, jnp.zeros((1, DB), F32))

    for k in ORDER:
        sent.append(send(in_buf.at[0], in_buf.at[k], in_s.at[k], in_r.at[k], dp, peer(k)))
    for step, other, to_dp, to_seq in replicas:
        sent.append(send(gu_rep.at[rep], gu_rep.at[rep], gr_s.at[step], gr_r.at[step], to_dp, to_seq))
        sent.append(send(dn_rep.at[rep], dn_rep.at[rep], dr_s.at[step], dr_r.at[step], to_dp, to_seq))

    for k in range(1, NB):
        arrived(in_buf.at[k], in_r.at[k])
    total = in_buf[0]
    for k in range(1, NB):
        total = total + in_buf[k]
    rows_ref[...] = total * (1.0 / width)

    sm_rep[rep] = jnp.zeros((BLK + SMALL, DB), F32)

    def backward(i, carry):
        q = 3 - i
        ks = [2 * q, 2 * q + 1, 2 * q + 8, 2 * q + 9]
        t_hi, t_lo = list(carry[:4]), list(carry[4:])
        gr = []
        for k in ks:
            inner = as_columns(rows_ref[pl.ds(xor(rank, k, 4), 1), :])
            sc = scb[k]
            gr.append(gb[k] + wsc[k] - resid[k] * sc * sc * sc * inner)
        fs = [first[k] for k in ks]
        mx = [mixed[k] for k in ks]
        gf = []
        for n in range(4):
            j, m = n % 2, n + 1 - 2 * (n % 2)
            gf.append(lo[j][0] * gr[n] + lo[1 - j][1] * gr[m])
            t_lo[2 * j] += jnp.sum(gr[n] * fs[n], axis=0, keepdims=True)
            t_lo[2 * j + 1] += jnp.sum(gr[n] * fs[m], axis=0, keepdims=True)
        for n in range(4):
            j, m = n // 2, (n + 2) % 4
            gm = hi[j][0] * gf[n] + hi[1 - j][1] * gf[m]
            t_hi[2 * j] += jnp.sum(gf[n] * mx[n], axis=0, keepdims=True)
            t_hi[2 * j + 1] += jnp.sum(gf[n] * mx[m], axis=0, keepdims=True)
            mh, ml = split(gm)
            gseq[ks[n]] = dot(back_left, jnp.concatenate([mh, mh, ml], axis=0), NN) + gr[n]
            k = ks[n]

            @pl.when(k != 0)
            def _():
                send(gseq.at[k], cols(out_x, rank), o_s.at[k], o_r.at[k], dp, peer(k))

            sm_rep[rep, :BLK, :] += dot(jnp.concatenate([mh, ml, mh], axis=1), right(xb[k], 1), NT)
        return tuple(t_hi + t_lo)

    zero = jnp.zeros((1, DB), F32)
    terms = lax.fori_loop(0, 4, backward, (zero,) * 8)
    own_x = pltpu.make_async_copy(gseq.at[0], cols(out_x, rank), o_r.at[0])
    own_x.start()
    for j in range(2):
        for c in range(2):
            place = 2 * (side_hi + j - 2 * side_hi * j) + c
            sm_rep[rep, pl.ds(BLK + place, 1), :] = terms[2 * j + c]
            place = 2 * (side_lo + j - 2 * side_lo * j) + c
            sm_rep[rep, pl.ds(BLK + 4 + place, 1), :] = terms[4 + 2 * j + c]
    sm_rep[rep, BLK + 8 : BLK + 9, :] = gain_sum
    for step, other, to_dp, to_seq in replicas:
        sent.append(send(sm_rep.at[rep], sm_rep.at[rep], sr_s.at[step], sr_r.at[step], to_dp, to_seq))

    for step, other, to_dp, to_seq in replicas:
        source = (rep + reps - step) % reps
        arrived(gu_rep.at[source], gr_r.at[step])
        arrived(dn_rep.at[source], dr_r.at[step])
    gu_sum, dn_sum = gu_rep[0], dn_rep[0]
    for other in range(1, reps):
        gu_sum = gu_sum + gu_rep[other]
        dn_sum = dn_sum + dn_rep[other]
    gu_f32[...] = gu_sum * factor
    dn_f32[...] = dn_sum.T * factor
    for s in range(count):
        gu_out[s] = gu_f32[s * rows : (s + 1) * rows, :]
        dn_out[s] = dn_f32[s * drows : (s + 1) * drows, :]
    for k in ORDER:
        sent.append(send(gu_out.at[peer(k)], out_gu.at[rank], go_s.at[k], go_r.at[k], dp, peer(k)))
        sent.append(send(dn_out.at[peer(k)], out_dn.at[rank], do_s.at[k], do_r.at[k], dp, peer(k)))
    own = [
        own_x,
        pltpu.make_async_copy(gu_out.at[me], out_gu.at[rank], go_r.at[0]),
        pltpu.make_async_copy(dn_out.at[me], out_dn.at[rank], do_r.at[0]),
    ]
    own[1].start()
    own[2].start()

    for step, other, to_dp, to_seq in replicas:
        source = (rep + reps - step) % reps
        arrived(sm_rep.at[source], sr_r.at[step])
    sm_sum = sm_rep[0]
    for other in range(1, reps):
        sm_sum = sm_sum + sm_rep[other]
    sm_tot[...] = sm_sum * factor
    part = BLK // NB

    def part_of(rk):
        return sm_tot.at[pl.ds(pl.multiple_of(rk * part, part), part), :]

    for k in ORDER:
        sent.append(send(part_of(xor(rank, k, 4)), bm_in.at[k], bm_s.at[k], bm_r.at[k], dp, peer(k)))
    bm_sum = sm_tot[pl.ds(pl.multiple_of(rank * part, part), part), :]
    for k in range(1, NB):
        arrived(bm_in.at[k], bm_r.at[k])
        bm_sum = bm_sum + bm_in[k]
    pack[0:part, :] = bm_sum
    pack[part : part + SMALL, :] = sm_tot[BLK : BLK + SMALL, :]
    for k in ORDER:
        sent.append(send(pack, out_small.at[rank], pk_s.at[k], pk_r.at[k], dp, peer(k)))
    own.append(pltpu.make_async_copy(pack, out_small.at[rank], pk_r.at[0]))
    own[3].start()

    for copy in own:
        copy.wait()
    for k in range(1, NB):
        source = xor(rank, k, 4)
        arrived(out_gu.at[source], go_r.at[k])
        arrived(out_dn.at[source], do_r.at[k])
        arrived(cols(out_x, source), o_r.at[k])
        arrived(out_small.at[source], pk_r.at[k])
        arrived(gseq.at[k], o_s.at[k])
    for copy in sent:
        copy.wait_send()


def per_device(inputs, cotangent, block_mix, twist_hi, twist_lo, gain, gate_up, down):
    tokens, width = inputs.shape[1:]
    count = lax.axis_size("seq")
    dps = lax.axis_size("dp")
    groups = count // NB
    reps = dps * groups
    rows, drows = gate_up.shape[0], down.shape[0]
    factor = 1.0 / math.sqrt(dps * count * tokens)
    gu_rows = jnp.transpose(gate_up, (2, 0, 1, 3)).reshape(NB, rows, 2 * FB)
    dn_rows = jnp.transpose(down, (1, 0, 2))
    vmem = pl.BlockSpec(memory_space=pltpu.VMEM)
    hbm = pl.BlockSpec(memory_space=pl.ANY)
    dma = pltpu.SemaphoreType.DMA
    part = BLK // NB
    field = pltpu.VMEM((NB, tokens, DB), F32)
    many = max(count, reps)
    out_x, out_gu, out_dn, out_small = pl.pallas_call(
        functools.partial(kernel, dps, count, factor),
        out_shape=(
            jax.ShapeDtypeStruct((tokens, width), F32),
            jax.ShapeDtypeStruct((NB, rows, 2 * FB), F32),
            jax.ShapeDtypeStruct((NB, drows, DB), F32),
            jax.ShapeDtypeStruct((NB, part + SMALL, DB), F32),
        ),
        in_specs=[hbm, hbm, hbm, hbm, vmem, vmem, vmem, vmem],
        out_specs=(hbm, hbm, hbm, hbm),
        scratch_shapes=[field] * 8
        + [
            pltpu.VMEM((count, rows, 2 * FB), F32),
            pltpu.VMEM((count, drows, DB), F32),
            pltpu.VMEM((DB, 2 * FB), F32),
            pltpu.VMEM((FB, DB), F32),
            pltpu.VMEM((3 * DB, 2 * FB), BF16),
            pltpu.VMEM((DB, 6 * FB), BF16),
            pltpu.VMEM((FB, 3 * DB), BF16),
            pltpu.VMEM((reps, DB, 2 * FB), F32),
            pltpu.VMEM((reps, DB, FB), F32),
            pltpu.VMEM((count, rows, 2 * FB), F32),
            pltpu.VMEM((count, drows, DB), F32),
            pltpu.VMEM((reps, BLK + SMALL, DB), F32),
            pltpu.VMEM((BLK + SMALL, DB), F32),
            pltpu.VMEM((NB, part, DB), F32),
            pltpu.VMEM((part + SMALL, DB), F32),
            pltpu.VMEM((NB, NB, BLK), F32),
            pltpu.VMEM((NB, NB, BLK), F32),
            pltpu.VMEM((NB, BLK), F32),
        ]
        + [dma((many,))] * 28,
        compiler_params=pltpu.CompilerParams(
            collective_id=0, has_side_effects=True, vmem_limit_bytes=50 * 1024 * 1024
        ),
        name="butterfly_block",
    )(inputs[0], cotangent[0], gu_rows, dn_rows, block_mix, twist_hi, twist_lo, gain.reshape(1, width))
    grad_gu = jnp.transpose(out_gu.reshape(NB, rows, 2, FB), (1, 2, 0, 3))
    grad_dn = jnp.transpose(out_dn, (1, 0, 2))
    small = jnp.transpose(out_small[:, part:], (1, 0, 2)).reshape(SMALL, width)
    return (
        out_x[None],
        grad_gu,
        grad_dn,
        out_small[:, :part].reshape(BLK, BLK),
        small[0:4].reshape(2, 2, width),
        small[4:8].reshape(2, 2, width),
        small[8],
    )


def solution(mesh):
    return jax.shard_map(
        per_device,
        mesh=mesh,
        in_specs=(
            P("dp", "seq", None),
            P("dp", "seq", None),
            P(),
            P(),
            P(),
            P(),
            P("seq", None, None, None),
            P("seq", None, None),
        ),
        out_specs=(
            P("dp", "seq", None),
            P("seq", None, None, None),
            P("seq", None, None),
            P(),
            P(),
            P(),
            P(),
        ),
        check_vma=False,
    )
```

time: 600 us -> 136 us (0.23)
  waiting for transfers between devices: 496 us -> 0 us
  Pallas kernels: 0 us -> 126 us
  matrix products: 43.8 us -> 0 us
  other arithmetic: 21.6 us -> 0 us
  between operations: 14.5 us -> 0.73 us
  local copies, waits for them, and re-layouts: 17.7 us -> 8.24 us
  starting transfers between devices: 6.27 us -> 0 us
    psum x3 -> x0, waiting for transfers between devices: 257 us -> none  [the longest x2 230 us: per_device(): lax.psum((term_block, term_hi, term_lo, grad_gain_local), ('dp', 'seq'))]
    reduce_scatter x2 -> x0, waiting for transfers between devices: 137 us -> none  [the longest x1 76 us: per_device(): lax.psum_scatter(whole_gu, 'seq', scatter_dimension=0, tiled=True)]
    pallas_call x0 -> x1, Pallas kernels: none -> 126 us  [per_device(): pl.pallas_call(functools.partial(kernel, dps, count, factor), out_shape=(...]
    ppermute x4 -> x0, waiting for transfers between devices: 59.5 us -> none  [from_partner(): return lax.ppermute(block, axis, route)]
    dot_general x11 -> x0, matrix products: 43.8 us -> none  [the longest x1 6.39 us: per_device(): whole_down = jnp.einsum('tnf,tnd->fnd', cols, grad_blocks, precision=HIGH)]
    all_gather x2 -> x0, waiting for transfers between devices: 42.3 us -> none  [the longest x1 42.3 us: per_device(): lax.all_gather(gate_up, 'seq', axis=0, tiled=True)]
    mul x11 -> x0, other arithmetic: 10.8 us -> none  [the longest x1 1.67 us: per_device(): part_gu * factor]
    unnamed x55 -> x15, local copies, waits for them, and re-layouts: 12.2 us -> 3.7 us
  transfers between devices with their start and end apart: 11 -> 0, of which waited for: 8 -> 0; matrix products, arithmetic and copies ran while one was open for 9% -> 0% of each run, Pallas kernels for 0% -> 0%
where the time goes in v1:
time: 136 us; the launch traced here: 135 us
  Pallas kernels  126 us (93%)
  local copies, waits for them, and re-layouts  8.24 us (6%)
    pallas_call x1, Pallas kernels, per_device(): pl.pallas_call(functools.partial(kernel, dps, count, factor), out_shape=(...  126 us
    unnamed x15, local copies, waits for them, and re-layouts  3.7 us

profile of v1, /device:TPU:0, one launch (start us, length us, event | category | flops | bytes accessed | tf_op | source)
XLA Modules:
  0.0 135.4 jit_solution(13405066990968354383)
XLA Ops:
  0.6 0.0 copy-start.5
  0.6 1.1 copy.19
  1.8 0.0 copy-done.5
  1.8 0.0 copy-start.1
  1.8 0.0 copy-start.2
  1.8 0.0 copy-start.3
  1.8 0.0 copy-start.4
  1.9 0.7 copy-done.1
  2.6 0.0 copy-done.2
  2.6 0.0 copy-done.3
  2.6 0.0 copy-done.4
  2.6 0.0 copy-start
  2.7 1.2 copy-done
  3.9 126.5 %butterfly_block.1 = (f32[128,2048]{1,0:T(8,128)S(1)}, f32[16,8,512]{2,1,0:T(8,128)S(1)}, f32[16,16,128]{2,1,0:T(8,128)S(1)}, f32[16,24,128]{2,1,0:T(8,128)S(1)}) custom-call(f32[128,2048]{1,0:T(8,128)S(1)} %bitcast.20, f32[128,2048]{1,0:T(8,128)} %bitcast.26, f32[16,8,512]{2,1,0:T(8,128)S(1)} %bitcast.19, f32[16,16,128]{2,1,0:T(8,128)S(1)} %bitcast.22, ...), custom_call_target="tpu_custom_call" | custom-call | tf_op jit(solution)/shard_map/butterfly_block/pallas_call | solution.py:391
  130.4 0.6 reshape.43
  131.0 0.6 reshape.44
  131.7 0.6 slice.25
  132.3 0.6 slice_bitcast_fusion.1
  132.9 0.9 copy.27
  133.8 0.7 copy.24
  134.5 1.0 copy.30
  (5 shorter events, 0.1 us)
Async XLA Ops:
  0.6 1.2 copy-start.5
  1.8 0.8 copy-start.1
  1.8 0.8 copy-start.2
  1.8 0.8 copy-start.3
  1.8 0.8 copy-start.4
  2.6 1.2 copy-start

commit v2 on v1

--- a/solution.py
+++ b/solution.py
@@ -19,7 +19,7 @@
 NN = (((1,), (0,)), ((), ()))
 NT = (((1,), (1,)), ((), ()))
 TN = (((0,), (0,)), ((), ()))
-ORDER = (8, 4, 9, 12, 1, 13, 10, 5, 14, 2, 11, 6, 15, 3, 7)
+ORDER = (8, 1, 9, 2, 10, 3, 11, 4, 12, 5, 13, 6, 14, 7, 15)
 
 
 def xor(a, b, bits):
@@ -64,15 +64,15 @@
 
 def kernel(
     dps, count, factor,
-    x_hbm, g_hbm, gu_hbm, dn_hbm, bm_ref, th_ref, tl_ref, gain_ref,
+    x_hbm, g_hbm, gu_ref, dn_ref, bm_ref, th_ref, tl_ref, gain_ref,
     out_x, out_gu, out_dn, out_small,
     xb, gb, mixed, first, resid, scb, wsc, gseq,
-    gu_in, dn_in, gu_f32, dn_f32, gu_k, gu_n, dn_n,
-    gu_rep, dn_rep, gu_out, dn_out, sm_rep, sm_tot, bm_in, pack,
+    gu_blk, dn_blk, gu_in, dn_in, gu_f32, dn_f32, dn_t, gu_k, gu_n, dn_n,
+    gu_part, dn_part, gu_rep, dn_rep, gu_out, dn_out, sm_rep, sm_tot, bm_in, pack,
     ss_buf, in_buf, rows_ref,
     x_s, x_r, g_s, g_r, gu_s, gu_r, dn_s, dn_r, ss_s, ss_r, in_s, in_r,
     o_s, o_r, gr_s, gr_r, dr_s, dr_r, go_s, go_r, do_s, do_r, sr_s, sr_r,
-    bm_s, bm_r, pk_s, pk_r,
+    bm_s, bm_r, pk_s, pk_r, wx_s, wx_r,
 ):
     groups = count // NB
     bits = count.bit_length() - 1
@@ -83,6 +83,9 @@
     rank = me % 2 + me // (2 * groups) * 2
     group = me // 2 % groups
     rep = dp * groups + group
+    half = dp % 2
+    pair = dp + 1 - 2 * half
+    odd = (me + half) % 2
 
     def seq_of(rk, grp):
         return rk % 2 + grp * 2 + rk // 2 * 2 * groups
@@ -126,19 +129,35 @@
     local = [
         pltpu.make_async_copy(cols(x_hbm, rank), xb.at[0], x_r.at[0]),
         pltpu.make_async_copy(cols(g_hbm, rank), gb.at[0], g_r.at[0]),
-        pltpu.make_async_copy(gu_hbm.at[rank], gu_in.at[me], gu_r.at[0]),
-        pltpu.make_async_copy(dn_hbm.at[rank], dn_in.at[me], dn_r.at[0]),
     ]
     for copy in local:
         copy.start()
     for k in ORDER:
         sent.append(send(cols(x_hbm, xor(rank, k, 4)), xb.at[k], x_s.at[k], x_r.at[k], dp, peer(k)))
-    for j in range(1, count):
-        k = ORDER[j - 1] if count == NB else j
+
+    def weight_copies(k):
         to = xor(me, k, bits)
         block = to % 2 + to // (2 * groups) * 2
-        sent.append(send(gu_hbm.at[block], gu_in.at[me], gu_s.at[k], gu_r.at[k], dp, to))
-        sent.append(send(dn_hbm.at[block], dn_in.at[me], dn_s.at[k], dn_r.at[k], dp, to))
+        slot = me // 2
+        return [
+            pltpu.make_async_remote_copy(
+                src_ref=src.at[block], dst_ref=dst.at[half, slot], send_sem=ssem.at[k],
+                recv_sem=rsem.at[k], device_id=(dp, to), device_id_type=pl.DeviceIdType.MESH,
+            )
+            for src, dst, ssem, rsem in ((gu_blk, gu_in, gu_s, gu_r), (dn_blk, dn_in, dn_s, dn_r))
+        ]
+
+    @pl.when(odd == 0)
+    def _():
+        for n in range(NB):
+            for j in range(2):
+                gu_blk[n, :, j * FB : (j + 1) * FB] = gu_ref[:, j, n, :]
+            dn_blk[n] = dn_ref[:, n, :]
+        pltpu.make_async_copy(gu_blk.at[rank], gu_in.at[half, me // 2], gu_r.at[0]).start()
+        pltpu.make_async_copy(dn_blk.at[rank], dn_in.at[half, me // 2], dn_r.at[0]).start()
+        for j in range(1, count):
+            for copy in weight_copies(ORDER[j - 1] if count == NB else j):
+                copy.start()
 
     mix_left = left(bm_ref[...], 1)
     back_left = left(bm_ref[...].T, 1)
@@ -186,18 +205,23 @@
     for k in ORDER:
         sent.append(send(ss_buf.at[0], ss_buf.at[k], ss_s.at[k], ss_r.at[k], dp, peer(k)))
 
-    for k in range(count):
+    for j in range(count // 2):
+        k = 2 * j + odd
         owner = xor(me, k, bits)
-        arrived(gu_in.at[owner], gu_r.at[k])
-        arrived(dn_in.at[owner], dn_r.at[k])
+        arrived(gu_in.at[half, owner // 2], gu_r.at[k])
+        arrived(dn_in.at[half, owner // 2], dn_r.at[k])
+    sent.append(send(gu_in.at[half], gu_in.at[half], wx_s.at[0], wx_r.at[0], pair, me))
+    sent.append(send(dn_in.at[half], dn_in.at[half], wx_s.at[1], wx_r.at[1], pair, me))
+    arrived(gu_in.at[1 - half], wx_r.at[0])
+    arrived(dn_in.at[1 - half], wx_r.at[1])
     for s in range(count):
-        gu_f32[s * rows : (s + 1) * rows, :] = gu_in[s]
-        dn_f32[s * drows : (s + 1) * drows, :] = dn_in[s]
+        gu_f32[s * rows : (s + 1) * rows, :] = gu_in[s % 2, s // 2]
+        dn_f32[s * drows : (s + 1) * drows, :] = dn_in[s % 2, s // 2]
     gu_k[...] = right(gu_f32[...], 0)
     gu_n[...] = right(gu_f32[...], 1)
     dn_n[...] = right(dn_f32[...], 1)
-    gu_rep[rep] = jnp.zeros((DB, 2 * FB), F32)
-    dn_rep[rep] = jnp.zeros((DB, FB), F32)
+    gu_f32[...] = jnp.zeros((DB, 2 * FB), F32)
+    dn_t[...] = jnp.zeros((DB, FB), F32)
 
     for k in range(1, NB):
         arrived(ss_buf.at[k], ss_r.at[k])
@@ -232,11 +256,11 @@
         grad_gate = grad_hidden * up * sig * (1.0 + gate * (1.0 - sig))
         both_h, both_l = split(jnp.concatenate([grad_gate, grad_hidden * act], axis=1))
         grad_normed = dot(jnp.concatenate([both_h, both_l, both_h], axis=1), gu_n[...], NT)
-        gu_rep[rep] += dot(
+        gu_f32[...] += dot(
             jnp.concatenate([nh, nl, nh], axis=0),
             jnp.concatenate([both_h, both_h, both_l], axis=0), TN,
         )
-        dn_rep[rep] += dot(jnp.concatenate([gh, gl, gh], axis=0), hidden, TN)
+        dn_t[...] += dot(jnp.concatenate([gh, gl, gh], axis=0), hidden, TN)
         weighted = grad_normed * gain
         prod = weighted * res
         ws = weighted * scale
@@ -250,9 +274,16 @@
 
     for k in ORDER:
         sent.append(send(in_buf.at[0], in_buf.at[k], in_s.at[k], in_r.at[k], dp, peer(k)))
+    dn_f32[...] = dn_t[...].T
+    for s in range(count):
+        gu_part[s % 2, s // 2] = gu_f32[s * rows : (s + 1) * rows, :]
+        dn_part[s % 2, s // 2] = dn_f32[s * drows : (s + 1) * drows, :]
     for step, other, to_dp, to_seq in replicas:
-        sent.append(send(gu_rep.at[rep], gu_rep.at[rep], gr_s.at[step], gr_r.at[step], to_dp, to_seq))
-        sent.append(send(dn_rep.at[rep], dn_rep.at[rep], dr_s.at[step], dr_r.at[step], to_dp, to_seq))
+        theirs = to_dp % 2
+        sent.append(send(gu_part.at[theirs], gu_rep.at[rep], gr_s.at[step], gr_r.at[step], to_dp, to_seq))
+        sent.append(send(dn_part.at[theirs], dn_rep.at[rep], dr_s.at[step], dr_r.at[step], to_dp, to_seq))
+    gu_rep[rep] = gu_part[half]
+    dn_rep[rep] = dn_part[half]
 
     for k in range(1, NB):
         arrived(in_buf.at[k], in_r.at[k])
@@ -260,6 +291,48 @@
     for k in range(1, NB):
         total = total + in_buf[k]
     rows_ref[...] = total * (1.0 / width)
+
+    for step, other, to_dp, to_seq in replicas:
+        source = (rep + reps - step) % reps
+        arrived(gu_rep.at[source], gr_r.at[step])
+        arrived(dn_rep.at[source], dr_r.at[step])
+    gu_sum, dn_sum = gu_rep[0], dn_rep[0]
+    for other in range(1, reps):
+        gu_sum = gu_sum + gu_rep[other]
+        dn_sum = dn_sum + dn_rep[other]
+    gu_out[...] = gu_sum * factor
+    dn_out[...] = dn_sum * factor
+
+    def grad_copies(k):
+        to = peer(k)
+        return [
+            pltpu.make_async_remote_copy(
+                src_ref=src.at[to // 2], dst_ref=dst.at[rank], send_sem=ssem.at[k],
+                recv_sem=rsem.at[k], device_id=(dp, to), device_id_type=pl.DeviceIdType.MESH,
+            )
+            for src, dst, ssem, rsem in ((gu_out, out_gu, go_s, go_r), (dn_out, out_dn, do_s, do_r))
+        ]
+
+    swap = [
+        pltpu.make_async_remote_copy(
+            src_ref=ref, dst_ref=ref, send_sem=wx_s.at[n], recv_sem=wx_r.at[n],
+            device_id=(pair, me), device_id_type=pl.DeviceIdType.MESH,
+        )
+        for n, ref in ((2, out_gu), (3, out_dn))
+    ]
+
+    @pl.when(odd == 0)
+    def _():
+        pltpu.make_async_copy(gu_out.at[me // 2], out_gu.at[rank], go_r.at[0]).start()
+        pltpu.make_async_copy(dn_out.at[me // 2], out_dn.at[rank], do_r.at[0]).start()
+
+    for j in reversed(range(NB // 2)):
+        k = 2 * j + odd
+
+        @pl.when(k != 0)
+        def _():
+            for copy in grad_copies(k):
+                copy.start()
 
     sm_rep[rep] = jnp.zeros((BLK + SMALL, DB), F32)
 
@@ -310,29 +383,14 @@
     for step, other, to_dp, to_seq in replicas:
         sent.append(send(sm_rep.at[rep], sm_rep.at[rep], sr_s.at[step], sr_r.at[step], to_dp, to_seq))
 
-    for step, other, to_dp, to_seq in replicas:
-        source = (rep + reps - step) % reps
-        arrived(gu_rep.at[source], gr_r.at[step])
-        arrived(dn_rep.at[source], dr_r.at[step])
-    gu_sum, dn_sum = gu_rep[0], dn_rep[0]
-    for other in range(1, reps):
-        gu_sum = gu_sum + gu_rep[other]
-        dn_sum = dn_sum + dn_rep[other]
-    gu_f32[...] = gu_sum * factor
-    dn_f32[...] = dn_sum.T * factor
-    for s in range(count):
-        gu_out[s] = gu_f32[s * rows : (s + 1) * rows, :]
-        dn_out[s] = dn_f32[s * drows : (s + 1) * drows, :]
-    for k in ORDER:
-        sent.append(send(gu_out.at[peer(k)], out_gu.at[rank], go_s.at[k], go_r.at[k], dp, peer(k)))
-        sent.append(send(dn_out.at[peer(k)], out_dn.at[rank], do_s.at[k], do_r.at[k], dp, peer(k)))
-    own = [
-        own_x,
-        pltpu.make_async_copy(gu_out.at[me], out_gu.at[rank], go_r.at[0]),
-        pltpu.make_async_copy(dn_out.at[me], out_dn.at[rank], do_r.at[0]),
-    ]
-    own[1].start()
-    own[2].start()
+    @pl.when(odd == 0)
+    def _():
+        for k in range(NB):
+            source = xor(rank, k, 4)
+            arrived(out_gu.at[source], go_r.at[k])
+            arrived(out_dn.at[source], do_r.at[k])
+        for copy in swap:
+            copy.start()
 
     for step, other, to_dp, to_seq in replicas:
         source = (rep + reps - step) % reps
@@ -356,20 +414,39 @@
     pack[part : part + SMALL, :] = sm_tot[BLK : BLK + SMALL, :]
     for k in ORDER:
         sent.append(send(pack, out_small.at[rank], pk_s.at[k], pk_r.at[k], dp, peer(k)))
-    own.append(pltpu.make_async_copy(pack, out_small.at[rank], pk_r.at[0]))
-    own[3].start()
+    own = [own_x, pltpu.make_async_copy(pack, out_small.at[rank], pk_r.at[0])]
+    own[1].start()
 
     for copy in own:
         copy.wait()
     for k in range(1, NB):
         source = xor(rank, k, 4)
-        arrived(out_gu.at[source], go_r.at[k])
-        arrived(out_dn.at[source], do_r.at[k])
         arrived(cols(out_x, source), o_r.at[k])
         arrived(out_small.at[source], pk_r.at[k])
         arrived(gseq.at[k], o_s.at[k])
     for copy in sent:
         copy.wait_send()
+
+    @pl.when(odd == 0)
+    def _():
+        for copy in swap:
+            copy.wait_send()
+        for k in range(1, count):
+            for copy in weight_copies(k):
+                copy.wait_send()
+
+    @pl.when(odd == 1)
+    def _():
+        for copy in swap:
+            copy.wait_recv()
+
+    for j in range(NB // 2):
+        k = 2 * j + odd
+
+        @pl.when(k != 0)
+        def _():
+            for copy in grad_copies(k):
+                copy.wait_send()
 
 
 def per_device(inputs, cotangent, block_mix, twist_hi, twist_lo, gain, gate_up, down):
@@ -380,8 +457,6 @@
     reps = dps * groups
     rows, drows = gate_up.shape[0], down.shape[0]
     factor = 1.0 / math.sqrt(dps * count * tokens)
-    gu_rows = jnp.transpose(gate_up, (2, 0, 1, 3)).reshape(NB, rows, 2 * FB)
-    dn_rows = jnp.transpose(down, (1, 0, 2))
     vmem = pl.BlockSpec(memory_space=pltpu.VMEM)
     hbm = pl.BlockSpec(memory_space=pl.ANY)
     dma = pltpu.SemaphoreType.DMA
@@ -396,21 +471,26 @@
             jax.ShapeDtypeStruct((NB, drows, DB), F32),
             jax.ShapeDtypeStruct((NB, part + SMALL, DB), F32),
         ),
-        in_specs=[hbm, hbm, hbm, hbm, vmem, vmem, vmem, vmem],
+        in_specs=[hbm, hbm] + [vmem] * 6,
         out_specs=(hbm, hbm, hbm, hbm),
         scratch_shapes=[field] * 8
         + [
-            pltpu.VMEM((count, rows, 2 * FB), F32),
-            pltpu.VMEM((count, drows, DB), F32),
+            pltpu.VMEM((NB, rows, 2 * FB), F32),
+            pltpu.VMEM((NB, drows, DB), F32),
+            pltpu.VMEM((2, count // 2, rows, 2 * FB), F32),
+            pltpu.VMEM((2, count // 2, drows, DB), F32),
             pltpu.VMEM((DB, 2 * FB), F32),
             pltpu.VMEM((FB, DB), F32),
+            pltpu.VMEM((DB, FB), F32),
             pltpu.VMEM((3 * DB, 2 * FB), BF16),
             pltpu.VMEM((DB, 6 * FB), BF16),
             pltpu.VMEM((FB, 3 * DB), BF16),
-            pltpu.VMEM((reps, DB, 2 * FB), F32),
-            pltpu.VMEM((reps, DB, FB), F32),
-            pltpu.VMEM((count, rows, 2 * FB), F32),
-            pltpu.VMEM((count, drows, DB), F32),
+            pltpu.VMEM((2, count // 2, rows, 2 * FB), F32),
+            pltpu.VMEM((2, count // 2, drows, DB), F32),
+            pltpu.VMEM((reps, count // 2, rows, 2 * FB), F32),
+            pltpu.VMEM((reps, count // 2, drows, DB), F32),
+            pltpu.VMEM((count // 2, rows, 2 * FB), F32),
+            pltpu.VMEM((count // 2, drows, DB), F32),
             pltpu.VMEM((reps, BLK + SMALL, DB), F32),
             pltpu.VMEM((BLK + SMALL, DB), F32),
             pltpu.VMEM((NB, part, DB), F32),
@@ -419,12 +499,12 @@
             pltpu.VMEM((NB, NB, BLK), F32),
             pltpu.VMEM((NB, BLK), F32),
         ]
-        + [dma((many,))] * 28,
+        + [dma((many,))] * 30,
         compiler_params=pltpu.CompilerParams(
             collective_id=0, has_side_effects=True, vmem_limit_bytes=50 * 1024 * 1024
         ),
         name="butterfly_block",
-    )(inputs[0], cotangent[0], gu_rows, dn_rows, block_mix, twist_hi, twist_lo, gain.reshape(1, width))
+    )(inputs[0], cotangent[0], gate_up, down, block_mix, twist_hi, twist_lo, gain.reshape(1, width))
     grad_gu = jnp.transpose(out_gu.reshape(NB, rows, 2, FB), (1, 2, 0, 3))
     grad_dn = jnp.transpose(out_dn, (1, 0, 2))
     small = jnp.transpose(out_small[:, part:], (1, 0, 2)).reshape(SMALL, width)

time: 136 us -> 129 us (0.949)
  Pallas kernels: 126 us -> 117 us
  local copies, waits for them, and re-layouts: 8.24 us -> 11.2 us
    pallas_call x1, Pallas kernels: 126 us -> 117 us  [per_device(): pl.pallas_call(functools.partial(kernel, dps, count, factor), out_shape=(...]
    unnamed x15 -> x16, local copies, waits for them, and re-layouts: 3.7 us -> 7.79 us
where the time goes in v2:
time: 129 us; the launch traced here: 128 us
  Pallas kernels  117 us (91%)
  local copies, waits for them, and re-layouts  11.2 us (9%)
    pallas_call x1, Pallas kernels, per_device(): pl.pallas_call(functools.partial(kernel, dps, count, factor), out_shape=(...  117 us
    unnamed x16, local copies, waits for them, and re-layouts  7.79 us

profile of v2, /device:TPU:0, one launch (start us, length us, event | category | flops | bytes accessed | tf_op | source)
XLA Modules:
  0.0 128.4 jit_solution(9829685130766699304)
XLA Ops:
  0.6 0.0 copy-start
  0.6 1.2 copy-done
  1.9 0.0 copy-start.1
  1.9 0.9 copy-done.1
  2.8 0.0 copy-start.2
  2.8 0.9 copy-done.2
  3.7 0.0 copy-start.3
  3.7 0.8 copy-done.3
  4.6 0.0 copy-start.4
  4.6 0.8 copy-done.4
  5.3 0.0 copy-start.5
  5.3 0.8 copy-done.5
  6.1 0.0 copy-start.6
  6.1 0.7 copy-done.6
  6.8 116.5 %butterfly_block.1 = (f32[128,2048]{1,0:T(8,128)S(1)}, f32[16,8,512]{2,1,0:T(8,128)S(1)}, f32[16,16,128]{2,1,0:T(8,128)S(1)}, f32[16,24,128]{2,1,0:T(8,128)S(1)}) custom-call(f32[128,2048]{1,0:T(8,128)S(1)} %bitcast.14, f32[128,2048]{1,0:T(8,128)} %bitcast.19, f32[8,2,16,256]{3,2,1,0:T(8,128)S(1)} %copy-done.1, f32[16,16,128]{2,1,0:T(8,128)S(1)} %copy-done.2, ...), custom_call_target="tpu_custom_call" | custom-call | tf_op jit(solution)/shard_map/butterfly_block/pallas_call | solution.py:466
  123.4 0.6 reshape.39
  124.0 0.6 reshape.40
  124.6 0.6 slice.25
  125.2 0.6 slice_bitcast_fusion.1
  125.9 0.9 copy.22
  126.7 0.7 copy.20
  127.4 1.0 copy.24
  (4 shorter events, 0.0 us)
Async XLA Ops:
  0.6 1.2 copy-start
  1.9 0.9 copy-start.1
  2.8 0.9 copy-start.2
  3.7 0.8 copy-start.3
  4.6 0.8 copy-start.4
  5.3 0.8 copy-start.5
  6.1 0.7 copy-start.6

commit v3 on v2

--- a/solution.py
+++ b/solution.py
@@ -14,6 +14,8 @@
 FB = 256
 EPS = 1e-05
 SMALL = 16
+PIECES = 4
+VMEM_LIMIT = 60 * 1024 * 1024
 F32 = jnp.float32
 BF16 = jnp.bfloat16
 NN = (((1,), (0,)), ((), ()))
@@ -64,15 +66,16 @@
 
 def kernel(
     dps, count, factor,
-    x_hbm, g_hbm, gu_ref, dn_ref, bm_ref, th_ref, tl_ref, gain_ref,
+    x_hbm, g_hbm, gu_hbm, dn_hbm, bm_hbm, th_hbm, tl_hbm, gain_hbm,
     out_x, out_gu, out_dn, out_small,
     xb, gb, mixed, first, resid, scb, wsc, gseq,
+    gu_ref, dn_ref, bm_ref, th_ref, tl_ref, gain_ref,
     gu_blk, dn_blk, gu_in, dn_in, gu_f32, dn_f32, dn_t, gu_k, gu_n, dn_n,
     gu_part, dn_part, gu_rep, dn_rep, gu_out, dn_out, sm_rep, sm_tot, bm_in, pack,
     ss_buf, in_buf, rows_ref,
     x_s, x_r, g_s, g_r, gu_s, gu_r, dn_s, dn_r, ss_s, ss_r, in_s, in_r,
     o_s, o_r, gr_s, gr_r, dr_s, dr_r, go_s, go_r, do_s, do_r, sr_s, sr_r,
-    bm_s, bm_r, pk_s, pk_r, wx_s, wx_r,
+    bm_s, bm_r, pk_s, pk_r, wx_s, wx_r, p_r,
 ):
     groups = count // NB
     bits = count.bit_length() - 1
@@ -108,6 +111,20 @@
     for step in range(1, reps):
         other = (rep + step) % reps
         replicas.append((step, other, other // groups, seq_of(rank, other % groups)))
+
+    params = [
+        pltpu.make_async_copy(src, dst, p_r.at[n])
+        for n, (src, dst) in enumerate((
+            (bm_hbm, bm_ref), (gu_hbm, gu_ref), (dn_hbm, dn_ref),
+            (th_hbm, th_ref), (tl_hbm, tl_ref), (gain_hbm, gain_ref),
+        ))
+    ]
+    local = [
+        pltpu.make_async_copy(cols(x_hbm, rank), xb.at[0], x_r.at[0]),
+        pltpu.make_async_copy(cols(g_hbm, rank), gb.at[0], g_r.at[0]),
+    ]
+    for copy in params + local:
+        copy.start()
 
     barrier = pltpu.get_barrier_semaphore()
     met = 0
@@ -126,14 +143,11 @@
     pl.semaphore_wait(barrier, met)
 
     sent = []
-    local = [
-        pltpu.make_async_copy(cols(x_hbm, rank), xb.at[0], x_r.at[0]),
-        pltpu.make_async_copy(cols(g_hbm, rank), gb.at[0], g_r.at[0]),
-    ]
-    for copy in local:
-        copy.start()
     for k in ORDER:
         sent.append(send(cols(x_hbm, xor(rank, k, 4)), xb.at[k], x_s.at[k], x_r.at[k], dp, peer(k)))
+
+    for copy in params:
+        copy.wait()
 
     def weight_copies(k):
         to = xor(me, k, bits)
@@ -292,48 +306,6 @@
         total = total + in_buf[k]
     rows_ref[...] = total * (1.0 / width)
 
-    for step, other, to_dp, to_seq in replicas:
-        source = (rep + reps - step) % reps
-        arrived(gu_rep.at[source], gr_r.at[step])
-        arrived(dn_rep.at[source], dr_r.at[step])
-    gu_sum, dn_sum = gu_rep[0], dn_rep[0]
-    for other in range(1, reps):
-        gu_sum = gu_sum + gu_rep[other]
-        dn_sum = dn_sum + dn_rep[other]
-    gu_out[...] = gu_sum * factor
-    dn_out[...] = dn_sum * factor
-
-    def grad_copies(k):
-        to = peer(k)
-        return [
-            pltpu.make_async_remote_copy(
-                src_ref=src.at[to // 2], dst_ref=dst.at[rank], send_sem=ssem.at[k],
-                recv_sem=rsem.at[k], device_id=(dp, to), device_id_type=pl.DeviceIdType.MESH,
-            )
-            for src, dst, ssem, rsem in ((gu_out, out_gu, go_s, go_r), (dn_out, out_dn, do_s, do_r))
-        ]
-
-    swap = [
-        pltpu.make_async_remote_copy(
-            src_ref=ref, dst_ref=ref, send_sem=wx_s.at[n], recv_sem=wx_r.at[n],
-            device_id=(pair, me), device_id_type=pl.DeviceIdType.MESH,
-        )
-        for n, ref in ((2, out_gu), (3, out_dn))
-    ]
-
-    @pl.when(odd == 0)
-    def _():
-        pltpu.make_async_copy(gu_out.at[me // 2], out_gu.at[rank], go_r.at[0]).start()
-        pltpu.make_async_copy(dn_out.at[me // 2], out_dn.at[rank], do_r.at[0]).start()
-
-    for j in reversed(range(NB // 2)):
-        k = 2 * j + odd
-
-        @pl.when(k != 0)
-        def _():
-            for copy in grad_copies(k):
-                copy.start()
-
     sm_rep[rep] = jnp.zeros((BLK + SMALL, DB), F32)
 
     def backward(i, carry):
@@ -370,7 +342,51 @@
         return tuple(t_hi + t_lo)
 
     zero = jnp.zeros((1, DB), F32)
-    terms = lax.fori_loop(0, 4, backward, (zero,) * 8)
+    terms = lax.fori_loop(0, 2, backward, (zero,) * 8)
+
+    for step, other, to_dp, to_seq in replicas:
+        source = (rep + reps - step) % reps
+        arrived(gu_rep.at[source], gr_r.at[step])
+        arrived(dn_rep.at[source], dr_r.at[step])
+    gu_sum, dn_sum = gu_rep[0], dn_rep[0]
+    for other in range(1, reps):
+        gu_sum = gu_sum + gu_rep[other]
+        dn_sum = dn_sum + dn_rep[other]
+    gu_out[...] = gu_sum * factor
+    dn_out[...] = dn_sum * factor
+
+    def grad_copies(k):
+        to = peer(k)
+        return [
+            pltpu.make_async_remote_copy(
+                src_ref=src.at[to // 2], dst_ref=dst.at[rank], send_sem=ssem.at[k],
+                recv_sem=rsem.at[k], device_id=(dp, to), device_id_type=pl.DeviceIdType.MESH,
+            )
+            for src, dst, ssem, rsem in ((gu_out, out_gu, go_s, go_r), (dn_out, out_dn, do_s, do_r))
+        ]
+
+    swap = [
+        pltpu.make_async_remote_copy(
+            src_ref=ref, dst_ref=ref, send_sem=wx_s.at[n], recv_sem=wx_r.at[n],
+            device_id=(pair, me), device_id_type=pl.DeviceIdType.MESH,
+        )
+        for n, ref in ((2, out_gu), (3, out_dn))
+    ]
+
+    @pl.when(odd == 0)
+    def _():
+        pltpu.make_async_copy(gu_out.at[me // 2], out_gu.at[rank], go_r.at[0]).start()
+        pltpu.make_async_copy(dn_out.at[me // 2], out_dn.at[rank], do_r.at[0]).start()
+
+    for j in reversed(range(NB // 2)):
+        k = 2 * j + odd
+
+        @pl.when(k != 0)
+        def _():
+            for copy in grad_copies(k):
+                copy.start()
+
+    terms = lax.fori_loop(2, 4, backward, terms)
     own_x = pltpu.make_async_copy(gseq.at[0], cols(out_x, rank), o_r.at[0])
     own_x.start()
     for j in range(2):
@@ -447,6 +463,30 @@
         def _():
             for copy in grad_copies(k):
                 copy.wait_send()
+
+
+def lay_out(x_in, gu_in, dn_in, small, x_out, gu_out, dn_out, bm_out, th_out, tl_out, gain_out, sem):
+    rows = x_in.shape[0] // PIECES
+    copies = [
+        pltpu.make_async_copy(
+            x_in.at[n * rows : (n + 1) * rows], x_out.at[n * rows : (n + 1) * rows], sem.at[n]
+        )
+        for n in range(PIECES)
+    ]
+    for copy in copies:
+        copy.start()
+    part = BLK // NB
+    for n in range(NB):
+        lanes = slice(n * DB, (n + 1) * DB)
+        for j in range(2):
+            gu_out[:, j, n, :] = gu_in[n, :, j * FB : (j + 1) * FB]
+            th_out[j, :, lanes] = small[n, part + 2 * j : part + 2 * j + 2, :]
+            tl_out[j, :, lanes] = small[n, part + 4 + 2 * j : part + 6 + 2 * j, :]
+        dn_out[:, n, :] = dn_in[n]
+        bm_out[n * part : (n + 1) * part, :] = small[n, 0:part, :]
+        gain_out[:, lanes] = small[n, part + 8 : part + 9, :]
+    for copy in copies:
+        copy.wait()
 
 
 def per_device(inputs, cotangent, block_mix, twist_hi, twist_lo, gain, gate_up, down):
@@ -471,10 +511,16 @@
             jax.ShapeDtypeStruct((NB, drows, DB), F32),
             jax.ShapeDtypeStruct((NB, part + SMALL, DB), F32),
         ),
-        in_specs=[hbm, hbm] + [vmem] * 6,
+        in_specs=[pl.BlockSpec(memory_space=pltpu.HBM)] * 8,
         out_specs=(hbm, hbm, hbm, hbm),
         scratch_shapes=[field] * 8
         + [
+            pltpu.VMEM(gate_up.shape, F32),
+            pltpu.VMEM(down.shape, F32),
+            pltpu.VMEM(block_mix.shape, F32),
+            pltpu.VMEM(twist_hi.shape, F32),
+            pltpu.VMEM(twist_lo.shape, F32),
+            pltpu.VMEM((1, width), F32),
             pltpu.VMEM((NB, rows, 2 * FB), F32),
             pltpu.VMEM((NB, drows, DB), F32),
             pltpu.VMEM((2, count // 2, rows, 2 * FB), F32),
@@ -499,24 +545,28 @@
             pltpu.VMEM((NB, NB, BLK), F32),
             pltpu.VMEM((NB, BLK), F32),
         ]
-        + [dma((many,))] * 30,
+        + [dma((many,))] * 31,
         compiler_params=pltpu.CompilerParams(
-            collective_id=0, has_side_effects=True, vmem_limit_bytes=50 * 1024 * 1024
+            collective_id=0, has_side_effects=True, vmem_limit_bytes=VMEM_LIMIT
         ),
         name="butterfly_block",
     )(inputs[0], cotangent[0], gate_up, down, block_mix, twist_hi, twist_lo, gain.reshape(1, width))
-    grad_gu = jnp.transpose(out_gu.reshape(NB, rows, 2, FB), (1, 2, 0, 3))
-    grad_dn = jnp.transpose(out_dn, (1, 0, 2))
-    small = jnp.transpose(out_small[:, part:], (1, 0, 2)).reshape(SMALL, width)
-    return (
-        out_x[None],
-        grad_gu,
-        grad_dn,
-        out_small[:, :part].reshape(BLK, BLK),
-        small[0:4].reshape(2, 2, width),
-        small[4:8].reshape(2, 2, width),
-        small[8],
-    )
+    outs = pl.pallas_call(
+        lay_out,
+        out_shape=tuple(
+            jax.ShapeDtypeStruct(shape, F32)
+            for shape in (
+                (tokens, width), gate_up.shape, down.shape, block_mix.shape,
+                twist_hi.shape, twist_lo.shape, (1, width),
+            )
+        ),
+        in_specs=[hbm, vmem, vmem, vmem],
+        out_specs=(hbm,) + (vmem,) * 6,
+        scratch_shapes=[dma((PIECES,))],
+        compiler_params=pltpu.CompilerParams(vmem_limit_bytes=VMEM_LIMIT),
+        name="lay_out",
+    )(out_x, out_gu, out_dn, out_small)
+    return (outs[0][None],) + tuple(outs[1:6]) + (outs[6].reshape(width),)
 
 
 def solution(mesh):

time: 129 us -> 155 us (1.20)
  Pallas kernels: 117 us -> 154 us
  local copies, waits for them, and re-layouts: 11.2 us -> 0 us
    pallas_call x0 -> x1, Pallas kernels: none -> 34.8 us  [per_device(): pl.pallas_call(lay_out, out_shape=tuple((jax.ShapeDtypeStruct(shape, F32)...]
    unnamed x16 -> x0, local copies, waits for them, and re-layouts: 7.79 us -> none
    reshape x4 -> x0, local copies, waits for them, and re-layouts: 2.76 us -> none  [the longest x1 0.86 us: per_device(): grad_gu = jnp.transpose(out_gu.reshape(NB, rows, 2, FB), (1, 2, 0, 3))]
    pallas_call x1, Pallas kernels: 117 us -> 119 us  [per_device(): pl.pallas_call(functools.partial(kernel, dps, count, factor), out_shape=(...]
where the time goes in v3:
time: 155 us
  Pallas kernels  154 us (99%)
    pallas_call x1, Pallas kernels, per_device(): pl.pallas_call(functools.partial(kernel, dps, count, factor), out_shape=(...  119 us
    pallas_call x1, Pallas kernels, per_device(): pl.pallas_call(lay_out, out_shape=tuple((jax.ShapeDtypeStruct(shape, F32)...  34.8 us

profile of v3, /device:TPU:0, one launch (start us, length us, event | category | flops | bytes accessed | tf_op | source)
XLA Modules:
  0.0 154.6 jit_solution(15960692391416995448)
XLA Ops:
  0.6 119.2 %butterfly_block.1 = (f32[128,2048]{1,0:T(8,128)}, f32[16,8,512]{2,1,0:T(8,128)}, f32[16,16,128]{2,1,0:T(8,128)}, f32[16,24,128]{2,1,0:T(8,128)}) custom-call(f32[128,2048]{1,0:T(8,128)} %bitcast.5, f32[128,2048]{1,0:T(8,128)} %bitcast.6, f32[8,2,16,256]{3,2,1,0:T(8,128)} %gu_hbm.1, f32[16,16,128]{2,1,0:T(8,128)} %dn_hbm.1, f32[128,128]{1,0:T(8,128)} %bm_hbm.1, ...), custom_call_target="tpu_custom_call" | custom-call | tf_op jit(solution)/shard_map/butterfly_block/pallas_call | solution.py:506
  119.9 34.8 %lay_out.1 = (f32[128,2048]{1,0:T(8,128)}, f32[8,2,16,256]{3,2,1,0:T(8,128)}, f32[16,16,128]{2,1,0:T(8,128)}, f32[128,128]{1,0:T(8,128)}, f32[2,2,2048]{2,1,0:T(...) custom-call(f32[128,2048]{1,0:T(8,128)} %get-tuple-element.18.x_in, f32[16,8,512]{2,1,0:T(8,128)} %get-tuple-element.19.gu_in, ...), custom_call_target="tpu_custom_call" | custom-call | tf_op jit(solution)/shard_map/lay_out/pallas_call | solution.py:554

commit v4 on v3

--- a/solution.py
+++ b/solution.py
@@ -67,8 +67,8 @@
 def kernel(
     dps, count, factor,
     x_hbm, g_hbm, gu_hbm, dn_hbm, bm_hbm, th_hbm, tl_hbm, gain_hbm,
-    out_x, out_gu, out_dn, out_small,
-    xb, gb, mixed, first, resid, scb, wsc, gseq,
+    out_x, res_gu, res_dn, out_small,
+    out_gu, out_dn, xb, gb, mixed, first, resid, scb, wsc, gseq,
     gu_ref, dn_ref, bm_ref, th_ref, tl_ref, gain_ref,
     gu_blk, dn_blk, gu_in, dn_in, gu_f32, dn_f32, dn_t, gu_k, gu_n, dn_n,
     gu_part, dn_part, gu_rep, dn_rep, gu_out, dn_out, sm_rep, sm_tot, bm_in, pack,
@@ -456,6 +456,13 @@
         for copy in swap:
             copy.wait_recv()
 
+    results = [
+        pltpu.make_async_copy(out_gu, res_gu, p_r.at[0]),
+        pltpu.make_async_copy(out_dn, res_dn, p_r.at[1]),
+    ]
+    for copy in results:
+        copy.start()
+
     for j in range(NB // 2):
         k = 2 * j + odd
 
@@ -464,17 +471,24 @@
             for copy in grad_copies(k):
                 copy.wait_send()
 
-
-def lay_out(x_in, gu_in, dn_in, small, x_out, gu_out, dn_out, bm_out, th_out, tl_out, gain_out, sem):
+    for copy in results:
+        copy.wait()
+
+
+def lay_out(x_in, gu_in, dn_in, small, x_out, gu_out, dn_out, bm_out, th_out, tl_out, gain_out, field, in_sem, out_sem):
     rows = x_in.shape[0] // PIECES
-    copies = [
-        pltpu.make_async_copy(
-            x_in.at[n * rows : (n + 1) * rows], x_out.at[n * rows : (n + 1) * rows], sem.at[n]
-        )
-        for n in range(PIECES)
+    spans = [slice(n * rows, (n + 1) * rows) for n in range(PIECES)]
+    loads = [
+        pltpu.make_async_copy(x_in.at[at], field.at[at], in_sem.at[n]) for n, at in enumerate(spans)
     ]
-    for copy in copies:
+    stores = [
+        pltpu.make_async_copy(field.at[at], x_out.at[at], out_sem.at[n]) for n, at in enumerate(spans)
+    ]
+    for copy in loads:
         copy.start()
+    for load, store in zip(loads, stores):
+        load.wait()
+        store.start()
     part = BLK // NB
     for n in range(NB):
         lanes = slice(n * DB, (n + 1) * DB)
@@ -485,7 +499,7 @@
         dn_out[:, n, :] = dn_in[n]
         bm_out[n * part : (n + 1) * part, :] = small[n, 0:part, :]
         gain_out[:, lanes] = small[n, part + 8 : part + 9, :]
-    for copy in copies:
+    for copy in stores:
         copy.wait()
 
 
@@ -513,7 +527,11 @@
         ),
         in_specs=[pl.BlockSpec(memory_space=pltpu.HBM)] * 8,
         out_specs=(hbm, hbm, hbm, hbm),
-        scratch_shapes=[field] * 8
+        scratch_shapes=[
+            pltpu.VMEM((NB, rows, 2 * FB), F32),
+            pltpu.VMEM((NB, drows, DB), F32),
+        ]
+        + [field] * 8
         + [
             pltpu.VMEM(gate_up.shape, F32),
             pltpu.VMEM(down.shape, F32),
@@ -562,7 +580,7 @@
         ),
         in_specs=[hbm, vmem, vmem, vmem],
         out_specs=(hbm,) + (vmem,) * 6,
-        scratch_shapes=[dma((PIECES,))],
+        scratch_shapes=[pltpu.VMEM((tokens, width), F32), dma((PIECES,)), dma((PIECES,))],
         compiler_params=pltpu.CompilerParams(vmem_limit_bytes=VMEM_LIMIT),
         name="lay_out",
     )(out_x, out_gu, out_dn, out_small)

time: 155 us -> 125 us (0.81)
  Pallas kernels: 154 us -> 124 us
    pallas_call x1, Pallas kernels: 34.8 us -> 3.83 us  [per_device(): pl.pallas_call(lay_out, out_shape=tuple((jax.ShapeDtypeStruct(shape, F32)...]
where the time goes in v4:
time: 125 us; the launch traced here: 124 us
  Pallas kernels  124 us (99%)
    pallas_call x1, Pallas kernels, per_device(): pl.pallas_call(functools.partial(kernel, dps, count, factor), out_shape=(...  120 us
    pallas_call x1, Pallas kernels, per_device(): pl.pallas_call(lay_out, out_shape=tuple((jax.ShapeDtypeStruct(shape, F32)...  3.83 us

profile of v4, /device:TPU:0, one launch (start us, length us, event | category | flops | bytes accessed | tf_op | source)
XLA Modules:
  0.0 124.4 jit_solution(5364197450413814919)
XLA Ops:
  0.6 120.0 %butterfly_block.1 = (f32[128,2048]{1,0:T(8,128)}, f32[16,8,512]{2,1,0:T(8,128)}, f32[16,16,128]{2,1,0:T(8,128)}, f32[16,24,128]{2,1,0:T(8,128)}) custom-call(f32[128,2048]{1,0:T(8,128)} %bitcast.5, f32[128,2048]{1,0:T(8,128)} %bitcast.6, f32[8,2,16,256]{3,2,1,0:T(8,128)} %gu_hbm.1, f32[16,16,128]{2,1,0:T(8,128)} %dn_hbm.1, f32[128,128]{1,0:T(8,128)} %bm_hbm.1, ...), custom_call_target="tpu_custom_call" | custom-call | tf_op jit(solution)/shard_map/butterfly_block/pallas_call | solution.py:520
  120.6 3.8 %lay_out.1 = (f32[128,2048]{1,0:T(8,128)}, f32[8,2,16,256]{3,2,1,0:T(8,128)}, f32[16,16,128]{2,1,0:T(8,128)}, f32[128,128]{1,0:T(8,128)}, f32[2,2,2048]{2,1,0:T(...) custom-call(f32[128,2048]{1,0:T(8,128)} %get-tuple-element.18.x_in, f32[16,8,512]{2,1,0:T(8,128)} %get-tuple-element.19.gu_in, ...), custom_call_target="tpu_custom_call" | custom-call | tf_op jit(solution)/shard_map/lay_out/pallas_call | solution.py:572
